TPU v7x, 512 devices: a whole 4x4x16 slice. The times are simulated.
512 devices in a mesh: band: 16 (over z), fft: 32 (over x, y, core).
Axes of the slice: x: 4, y: 4, z: 16, core: 2. Of those that a mesh axis runs over, the one named last changes fastest.
Arguments:
- wave_coeffs: float32 [2, 16, 96, 4096], P(None, 'band', None, 'fft'), may hold values from -6 to 6
- correction: float32 [2, 16, 96, 4096], P(None, 'band', None, 'fft'), may hold values from -6 to 6
- kinetic: float32 [96, 4096], P(None, 'fft'), may hold values from 0.1 to 4
- z_slots: int32 [96, 4096], P(None, 'fft'), may hold values from 0 to 191, as said below
- stick_cols: int32 [2, 4096], replicated, may hold values from 0 to 191, as said below
- x_lines: int32 [96], replicated, may hold values from 0 to 191, as said below
- potential: float32 [192, 36864], P('fft'), may hold values from 0.5 to 3
Outputs:
- h_coeffs: float32 [2, 16, 96, 4096], P(None, 'band', None, 'fft')
- reduced: float32 [2, 16, 16], P(None, 'band')
Inputs may be any that keep to these rules, and one draw needn't show every extreme that they name: `x_lines`: the 96 x frequencies are distinct. `stick_cols`: no two sticks share both their x line and their y frequency. `z_slots`: the 96 z frequencies of a stick are distinct.
All inputs are finite; a program needn't handle non-finite values.
Results may differ from a plain program's by a relative error of at most 0.000098.
Values sent between devices are 32-bit elements; how exact they have to be, the bound alone decides.
A program may use at most 128 MiB of HBM per device.

v0:
```python
import functools
import math

import jax
import jax.numpy as jnp
import numpy as np
from jax import lax
from jax.experimental import pallas as pl
from jax.experimental.pallas import tpu as pltpu
from jax.sharding import PartitionSpec as P

MESH = pl.DeviceIdType.MESH
F32 = jnp.float32
BF16 = jnp.bfloat16
G = 192
GP = 256
L = 96
K = 96
SL = 128
NF = 32
NB = 16
PL = 6
CP = 12
CPP = 16
NP = 16


def halves(table):
    hi = table.astype(jnp.bfloat16)
    lo = (table - hi.astype(np.float64)).astype(jnp.bfloat16)
    return hi, lo


def tables():
    f = np.arange(G)
    angle = 2.0 * math.pi * ((f[:, None] * f[None, :]) % G) / G
    cos, sin = np.cos(angle), np.sin(angle)
    plane_cos = np.zeros((GP, GP))
    plane_sin = np.zeros((GP, GP))
    plane_cos[:G, :G] = cos
    plane_sin[:G, :G] = sin
    forward = np.zeros((NF, CPP, 2, G))
    for part in range(2):
        rows = slice(part * PL, part * PL + PL)
        by_owner_cos = cos.reshape(NF, PL, G)
        by_owner_sin = sin.reshape(NF, PL, G)
        forward[:, rows, 0] = by_owner_sin if part else by_owner_cos
        forward[:, rows, 1] = by_owner_cos if part else -by_owner_sin
    forward = forward.reshape(NF * CPP, 2 * G)
    back = np.ascontiguousarray(forward.T)
    plane = np.stack(halves(plane_cos) + halves(plane_sin))
    return plane, np.stack(halves(forward)), np.stack(halves(back))


def split(value):
    hi = value.astype(BF16)
    lo = (value - hi.astype(F32)).astype(BF16)
    return hi, lo


def dot(a, b):
    return jnp.dot(a, b, preferred_element_type=F32)


def dot_nt(a, b):
    return lax.dot_general(a, b, (((1,), (1,)), ((), ())), preferred_element_type=F32)


def dot3(ah, al, bh, bl):
    return dot(ah, bh) + dot(al, bh) + dot(ah, bl)


def kernel(
    wave,
    corr,
    kinetic,
    zslots,
    sticks,
    xline,
    pot,
    plane_tab,
    fwd_tab,
    back_tab,
    h_out,
    red_out,
    send1,
    recv1,
    send2,
    recv2,
    dense,
    corr_all,
    potr,
    qt,
    pm,
    lhs_h,
    lhs_l,
    acc,
    s1h,
    s1l,
    s3h,
    s3l,
    o4h,
    o4l,
    back,
    ered,
    fsum,
    bsum,
    s1_send,
    s1_recv,
    s2_send,
    s2_recv,
    up_send,
    up_recv,
    dn_send,
    dn_recv,
    f_send,
    f_recv,
    b_send,
    b_recv,
):
    band = lax.axis_index("band")
    fft = lax.axis_index("fft")
    barrier = pltpu.get_barrier_semaphore()

    def to_fft(d):
        return {"fft": d}

    def to_band(d):
        return {"band": d}

    recv2[...] = jnp.zeros(recv2.shape, F32)

    def greet_fft(t, carry):
        d = lax.rem(fft + t, NF)
        pl.semaphore_signal(barrier, inc=1, device_id=to_fft(d), device_id_type=MESH)
        return carry

    def greet_band(t, carry):
        d = lax.rem(band + t, NB)
        pl.semaphore_signal(barrier, inc=1, device_id=to_band(d), device_id_type=MESH)
        return carry

    lax.fori_loop(1, NF, greet_fft, 0)
    lax.fori_loop(1, NB, greet_band, 0)

    corr_all[band] = corr[:, 0]

    def z_half(start):
        iota = lax.broadcasted_iota(jnp.int32, (G // 2, SL), 0) + start

        def step(k, carry):
            re, im = carry
            row = zslots[pl.ds(k, 1), :]
            hit = iota == row
            re = jnp.where(hit, wave[0, 0, pl.ds(k, 1), :], re)
            im = jnp.where(hit, wave[1, 0, pl.ds(k, 1), :], im)
            return re, im

        zero = jnp.zeros((G // 2, SL), F32)
        re, im = lax.fori_loop(0, K, step, (zero, zero), unroll=4)
        dense[pl.ds(start, G // 2), :] = re
        dense[pl.ds(G + start, G // 2), :] = im

    z_half(0)
    z_half(G // 2)
    dh, dl = split(dense[...])
    send1[...] = dot3(fwd_tab[0], fwd_tab[1], dh, dl).reshape(NF, CPP, SL)

    pl.semaphore_wait(barrier, NF - 1 + NB - 1)

    def copy1(dst, src):
        return pltpu.make_async_remote_copy(
            src_ref=send1.at[dst, pl.ds(0, CP)],
            dst_ref=recv1.at[src, pl.ds(0, CP)],
            send_sem=s1_send.at[dst],
            recv_sem=s1_recv.at[src],
            device_id=to_fft(dst),
            device_id_type=MESH,
        )

    def copy2(dst, src):
        return pltpu.make_async_remote_copy(
            src_ref=send2.at[dst, pl.ds(0, CP)],
            dst_ref=recv2.at[src, pl.ds(0, CP)],
            send_sem=s2_send.at[dst],
            recv_sem=s2_recv.at[src],
            device_id=to_fft(dst),
            device_id_type=MESH,
        )

    def send_one(t, carry):
        copy1(lax.rem(fft + t, NF), fft).start()
        return carry

    lax.fori_loop(1, NF, send_one, 0)
    recv1[fft] = send1[fft]

    above = lax.rem(band + 1, NB)
    below = lax.rem(band + NB - 1, NB)

    def up_copy(t):
        slot = lax.rem(band - t + 1 + NB, NB)
        return pltpu.make_async_remote_copy(
            src_ref=corr_all.at[slot],
            dst_ref=corr_all.at[slot],
            send_sem=up_send.at[t - 1],
            recv_sem=up_recv.at[t - 1],
            device_id=to_band(above),
            device_id_type=MESH,
        )

    def down_copy(t):
        slot = lax.rem(band + t - 1, NB)
        return pltpu.make_async_remote_copy(
            src_ref=corr_all.at[slot],
            dst_ref=corr_all.at[slot],
            send_sem=dn_send.at[t - 1],
            recv_sem=dn_recv.at[t - 1],
            device_id=to_band(below),
            device_id_type=MESH,
        )

    def ring(t):
        if t > 1:
            up_copy(t - 1).wait_recv()
        if t <= 8:
            up_copy(t).start()
        if 1 < t <= 8:
            down_copy(t - 1).wait_recv()
        if t <= 7:
            down_copy(t).start()

    ring(1)

    y_iota = lax.broadcasted_iota(jnp.int32, (GP, GP), 0)
    l_iota = lax.broadcasted_iota(jnp.int32, (L, GP), 0)

    def one_hots(t, carry):
        lane = pl.ds(pl.multiple_of(t * GP, GP), GP)
        hit = y_iota == sticks[1:2, lane]
        qt[t] = jnp.where(hit, 1.0, 0.0).astype(BF16)
        line = l_iota == sticks[0:1, lane]
        pm[t] = jnp.where(line, 1.0, 0.0).astype(BF16)
        return carry

    lax.fori_loop(0, NP, one_hots, 0)

    potr[...] = jnp.zeros(potr.shape, F32)

    def relay(q, carry):
        block = pot[:, pl.ds(pl.multiple_of(q * 2 * G, SL), 2 * G)]
        even = block[:, :G]
        odd = block[:, G:]
        for p in range(PL):
            potr[p, pl.ds(2 * q, 1), 0:G] = even[p : p + 1]
            potr[p, pl.ds(2 * q + 1, 1), 0:G] = odd[p : p + 1]
        return carry

    lax.fori_loop(0, G // 2, relay, 0)

    ered[...] = jnp.zeros(ered.shape, F32)
    ered[:, 0:L] = jnp.where(
        lax.broadcasted_iota(jnp.int32, (GP, L), 0) == xline[...], 1.0, 0.0
    )
    pick = ered[...]
    pick_b = pick.astype(BF16)
    pick_t = jnp.transpose(pick)[:L].astype(BF16)
    ch, cl, sh, sl = plane_tab[0], plane_tab[1], plane_tab[2], plane_tab[3]

    def x_tables(c, s):
        xc = dot(c[:G], pick_b).astype(BF16)
        xs = dot(s[:G], pick_b).astype(BF16)
        forward = jnp.concatenate(
            [
                jnp.concatenate([xc, -xs], axis=1),
                jnp.concatenate([xs, xc], axis=1),
            ],
            axis=0,
        )
        yc = dot(pick_t, c)[:, :G].astype(BF16)
        ys = dot(pick_t, s)[:, :G].astype(BF16)
        back_re = jnp.concatenate([yc, -ys], axis=0)
        back_im = jnp.concatenate([ys, yc], axis=0)
        return forward, back_re, back_im

    xf_h, xr_h, xi_h = x_tables(ch, sh)
    xf_l, xr_l, xi_l = x_tables(cl, sl)

    acc[...] = jnp.zeros(acc.shape, F32)
    my_pair = fft // 2

    def scatter_step(t, carry):
        pair = lax.rem(my_pair + t, NP)
        a = 2 * pair
        b = a + 1

        @pl.when(a != fft)
        def _():
            copy1(a, a).wait_recv()

        @pl.when(b != fft)
        def _():
            copy1(b, b).wait_recv()

        x = jnp.concatenate([recv1[a], recv1[b]], axis=1)
        mask = pm[pair]
        for cp in range(CP):
            row = jnp.broadcast_to(x[cp : cp + 1], (16, GP))
            hi, lo = split(row)
            lhs_h[cp * L : cp * L + L] = (mask.reshape(L // 16, 16, GP) * hi[None]).reshape(L, GP)
            lhs_l[cp * L : cp * L + L] = (mask.reshape(L // 16, 16, GP) * lo[None]).reshape(L, GP)
        q = qt[pair]
        acc[...] += dot_nt(lhs_h[...], q) + dot_nt(lhs_l[...], q)
        return carry

    lax.fori_loop(0, 6, scatter_step, 0)
    ring(2)
    lax.fori_loop(6, NP, scatter_step, 0)
    ring(3)

    s1h[...] = jnp.zeros(s1h.shape, BF16)
    s1l[...] = jnp.zeros(s1l.shape, BF16)
    half = PL * L

    def y_forward(p, carry):
        re_h, re_l = split(acc[pl.ds(p * L, L), :])
        im_h, im_l = split(acc[pl.ds(half + p * L, L), :])
        ah = jnp.concatenate([re_h, im_h], axis=0)
        al = jnp.concatenate([re_l, im_l], axis=0)
        u = dot3(ah, al, ch, cl)
        v = dot3(ah, al, sh, sl)
        hi, lo = split(u[:L] - v[L:])
        s1h[p, 0:L] = hi
        s1l[p, 0:L] = lo
        hi, lo = split(v[:L] + u[L:])
        s1h[p, SL : SL + L] = hi
        s1l[p, SL : SL + L] = lo
        return carry

    lax.fori_loop(0, PL, y_forward, 0)
    ring(4)

    def x_both(p, carry):
        r = dot3(xf_h, xf_l, s1h[p], s1l[p])
        v = potr[p]
        re_h, re_l = split(r[:G] * v)
        im_h, im_l = split(r[G:] * v)
        s = dot3(xr_h, xr_l, re_h, re_l) + dot3(xi_h, xi_l, im_h, im_l)
        hi, lo = split(s)
        s3h[p] = hi
        s3l[p] = lo
        return carry

    lax.fori_loop(0, 3, x_both, 0)
    ring(5)
    lax.fori_loop(3, PL, x_both, 0)
    ring(6)

    def y_back(p, carry):
        ah, al = s3h[p], s3l[p]
        u = dot3(ah, al, ch, cl)
        v = dot3(ah, al, sh, sl)
        hi, lo = split(u[:L] + v[L:])
        o4h[pl.ds(p * L, L), :] = hi
        o4l[pl.ds(p * L, L), :] = lo
        hi, lo = split(u[L:] - v[:L])
        o4h[pl.ds(half + p * L, L), :] = hi
        o4l[pl.ds(half + p * L, L), :] = lo
        return carry

    lax.fori_loop(0, PL, y_back, 0)
    ring(7)

    def gather_step(t, carry):
        pair = lax.rem(my_pair + t, NP)
        a = 2 * pair
        b = a + 1
        q = qt[pair]
        lane = pl.ds(pl.multiple_of(pair * GP, GP), GP)
        line = l_iota == sticks[0:1, lane]
        full = dot(o4h[...], q) + dot(o4l[...], q)
        for cp in range(CP):
            v = jnp.sum(jnp.where(line, full[cp * L : cp * L + L], 0.0), axis=0, keepdims=True)
            send2[a, cp : cp + 1, :] = v[:, :SL]
            send2[b, cp : cp + 1, :] = v[:, SL:]

        @pl.when(a != fft)
        def _():
            copy2(a, fft).start()

        @pl.when(b != fft)
        def _():
            copy2(b, fft).start()

        return carry

    lax.fori_loop(1, 8, gather_step, 0)
    ring(8)
    lax.fori_loop(8, NP + 1, gather_step, 0)
    recv2[fft, 0:CP] = send2[fft, 0:CP]
    ring(9)

    def wait_two(t, carry):
        src = lax.rem(fft + t, NF)
        copy2(src, src).wait_recv()
        return carry

    lax.fori_loop(1, NF, wait_two, 0)

    bh, bl = split(recv2[...].reshape(NF * CPP, SL))
    back[...] = dot3(back_tab[0], back_tab[1], bh, bl)
    zs = zslots[...]

    def pick_step(z, carry):
        re, im = carry
        hit = zs == z
        re = jnp.where(hit, back[pl.ds(z, 1), :], re)
        im = jnp.where(hit, back[pl.ds(G + z, 1), :], im)
        return re, im

    zero = jnp.zeros((K, SL), F32)
    v_re, v_im = lax.fori_loop(0, G, pick_step, (zero, zero), unroll=4)
    scale = 1.0 / float(G) ** 3
    kin = kinetic[...]
    h_re = kin * wave[0, 0] + v_re * scale
    h_im = kin * wave[1, 0] + v_im * scale
    h_out[0, 0] = h_re
    h_out[1, 0] = h_im

    row_iota = lax.broadcasted_iota(jnp.int32, (2 * NB, SL), 0)

    def contract(i, total):
        c_re = corr_all[i, 0]
        c_im = corr_all[i, 1]
        re = jnp.sum(c_re * h_re + c_im * h_im, axis=0, keepdims=True)
        im = jnp.sum(c_re * h_im - c_im * h_re, axis=0, keepdims=True)
        total = jnp.where(row_iota == i, re, total)
        return jnp.where(row_iota == NB + i, im, total)

    total = lax.fori_loop(0, NB, contract, jnp.zeros((2 * NB, SL), F32))
    column = jnp.sum(total, axis=1, keepdims=True)
    lane_iota = lax.broadcasted_iota(jnp.int32, (2 * NB, SL), 1)
    mine = jnp.sum(jnp.where(row_iota == lane_iota, column, 0.0), axis=0, keepdims=True)
    fsum[fft] = mine

    def f_copy(dst, src):
        return pltpu.make_async_remote_copy(
            src_ref=fsum.at[src],
            dst_ref=fsum.at[src],
            send_sem=f_send.at[dst],
            recv_sem=f_recv.at[src],
            device_id=to_fft(dst),
            device_id_type=MESH,
        )

    def b_copy(dst, src):
        return pltpu.make_async_remote_copy(
            src_ref=bsum.at[src],
            dst_ref=bsum.at[src],
            send_sem=b_send.at[dst],
            recv_sem=b_recv.at[src],
            device_id=to_band(dst),
            device_id_type=MESH,
        )

    def f_start(t, carry):
        f_copy(lax.rem(fft + t, NF), fft).start()
        return carry

    def f_wait(t, carry):
        src = lax.rem(fft + t, NF)
        f_copy(src, src).wait_recv()
        return carry

    lax.fori_loop(1, NF, f_start, 0)
    lax.fori_loop(1, NF, f_wait, 0)
    bsum[band] = jnp.sum(fsum[...], axis=0)

    def b_start(t, carry):
        b_copy(lax.rem(band + t, NB), band).start()
        return carry

    def b_wait(t, carry):
        src = lax.rem(band + t, NB)
        b_copy(src, src).wait_recv()
        return carry

    lax.fori_loop(1, NB, b_start, 0)
    lax.fori_loop(1, NB, b_wait, 0)

    block = bsum[...].reshape(NB, SL)
    root = 1.0 / math.sqrt(NF * SL * K)
    b_row = lax.broadcasted_iota(jnp.int32, (NB, SL), 0)
    b_lane = lax.broadcasted_iota(jnp.int32, (NB, SL), 1)
    for part in range(2):
        column = jnp.sum(
            jnp.where(b_lane == part * NB + band, block, 0.0), axis=1, keepdims=True
        )
        line = jnp.sum(jnp.where(b_row == b_lane, column, 0.0), axis=0, keepdims=True)
        red_out[part] = line[:, :NB] * root

    def drain(t, carry):
        d = lax.rem(fft + t, NF)
        copy1(d, fft).wait_send()
        copy2(d, fft).wait_send()
        f_copy(d, fft).wait_send()
        return carry

    lax.fori_loop(1, NF, drain, 0)

    def drain_band(t, carry):
        b_copy(lax.rem(band + t, NB), band).wait_send()
        return carry

    lax.fori_loop(1, NB, drain_band, 0)
    for t in range(1, 9):
        up_copy(t).wait_send()
        if t <= 7:
            down_copy(t).wait_send()


def local(wave, corr, kinetic, zslots, sticks, xlines, pot):
    plane, forward, back = tables()
    dma = pltpu.SemaphoreType.DMA
    vmem = pltpu.VMEM
    return pl.pallas_call(
        kernel,
        out_shape=(
            jax.ShapeDtypeStruct((2, 1, K, SL), F32),
            jax.ShapeDtypeStruct((2, 1, NB), F32),
        ),
        in_specs=[pl.BlockSpec(memory_space=vmem)] * 10,
        out_specs=(pl.BlockSpec(memory_space=vmem),) * 2,
        scratch_shapes=[
            vmem((NF, CPP, SL), F32),
            vmem((NF, CPP, SL), F32),
            vmem((NF, CPP, SL), F32),
            vmem((NF, CPP, SL), F32),
            vmem((2 * G, SL), F32),
            vmem((NB, 2, K, SL), F32),
            vmem((PL, G, GP), F32),
            vmem((NP, GP, GP), BF16),
            vmem((NP, L, GP), BF16),
            vmem((CP * L, GP), BF16),
            vmem((CP * L, GP), BF16),
            vmem((CP * L, GP), F32),
            vmem((PL, GP, GP), BF16),
            vmem((PL, GP, GP), BF16),
            vmem((PL, 2 * L, GP), BF16),
            vmem((PL, 2 * L, GP), BF16),
            vmem((CP * L, GP), BF16),
            vmem((CP * L, GP), BF16),
            vmem((2 * G, SL), F32),
            vmem((GP, SL), F32),
            vmem((NF, 1, SL), F32),
            vmem((NB, 1, SL), F32),
            dma((NF,)),
            dma((NF,)),
            dma((NF,)),
            dma((NF,)),
            dma((8,)),
            dma((8,)),
            dma((8,)),
            dma((8,)),
            dma((NF,)),
            dma((NF,)),
            dma((NB,)),
            dma((NB,)),
        ],
        compiler_params=pltpu.CompilerParams(
            collective_id=0,
            has_side_effects=True,
            vmem_limit_bytes=48 * 1024 * 1024,
        ),
    )(
        wave,
        corr,
        kinetic,
        zslots,
        sticks,
        xlines.reshape(1, L),
        pot,
        jnp.asarray(plane),
        jnp.asarray(forward),
        jnp.asarray(back),
    )


def solution(mesh):
    return jax.shard_map(
        local,
        mesh=mesh,
        in_specs=(
            P(None, "band", None, "fft"),
            P(None, "band", None, "fft"),
            P(None, "fft"),
            P(None, "fft"),
            P(),
            P(),
            P("fft", None),
        ),
        out_specs=(P(None, "band", None, "fft"), P(None, "band", None)),
        check_vma=False,
    )
```

profile of v0, /device:TPU:1, one launch (start us, length us, event | category | flops | bytes accessed | tf_op | source)
XLA Modules:
  0.0 90.9 jit_solution(15503324654001535170)
XLA Ops:
  0.6 0.0 copy-start
  0.6 1.3 %copy-done = f32[6,36864]{1,0:T(8,128)S(1)} copy-done((f32[6,36864]{1,0:T(8,128)S(1)}, f32[6,36864]{1,0:T(8,128)}, u32[]{:S(2)}) %copy-start) | copy-done | bytes 884760
  1.9 0.0 copy-start.1
  1.9 1.1 %copy-done.1 = bf16[2,384,512]{2,1,0:T(8,128)(2,1)S(1)} copy-done((bf16[2,384,512]{2,1,0:T(8,128)(2,1)S(1)}, bf16[2,384,512]{2,1,0:T(8,128)(2,1)}, u32[]{:S(2)}) %copy-start.1) | copy-done | bytes 786456
  3.0 0.0 copy-start.2
  3.0 1.1 %copy-done.2 = bf16[2,512,384]{2,1,0:T(8,128)(2,1)S(1)} copy-done((bf16[2,512,384]{2,1,0:T(8,128)(2,1)S(1)}, bf16[2,512,384]{2,1,0:T(8,128)(2,1)}, u32[]{:S(2)}) %copy-start.2) | copy-done | bytes 786456
  4.2 0.0 copy-start.3
  4.2 1.0 %copy-done.3 = bf16[4,256,256]{2,1,0:T(8,128)(2,1)S(1)} copy-done((bf16[4,256,256]{2,1,0:T(8,128)(2,1)S(1)}, bf16[4,256,256]{2,1,0:T(8,128)(2,1)}, u32[]{:S(2)}) %copy-start.3) | copy-done | bytes 524312
  5.2 0.0 copy-start.4
  5.2 0.9 copy-done.4
  6.1 0.0 copy-start.5
  6.1 0.9 copy-done.5
  7.0 0.0 copy-start.6
  7.0 0.8 copy-done.6
  7.8 0.0 copy-start.7
  7.8 0.8 copy-done.7
  8.6 0.0 copy-start.8
  8.6 0.8 copy-done.8
  9.4 0.0 copy-start.9
  9.4 0.7 copy-done.9
  10.0 79.7 %shard_map.113 = (f32[2,1,96,128]{3,2,1,0:T(8,128)S(1)}, f32[2,1,16]{2,1,0:T(1,128)S(1)}) custom-call(f32[2,1,96,128]{3,2,1,0:T(8,128)S(1)} %copy-done.4, f32[2,1,96,128]{3,2,1,0:T(8,128)S(1)} %copy-done.5, f32[96,128]{1,0:T(8,128)S(1)} %copy-done.6, s32[96,128]{1,0:T(8,128)S(1)} %copy-done.7, s32[2,4096]{1,0:T(2,128)S(1)} %copy-done.8, ...), custom_call_target="tpu_custom_call" | custom-call | tf_op jit(solution)/shard_map/pallas_call | solution.py:526
  89.7 0.6 copy.14
  90.4 0.6 copy.15
Async XLA Ops:
  0.6 1.3 %copy-start = (f32[6,36864]{1,0:T(8,128)S(1)}, f32[6,36864]{1,0:T(8,128)}, u32[]{:S(2)}) copy-start(f32[6,36864]{1,0:T(8,128)} %pot.1) | copy-start | bytes 2654212
  1.9 1.1 %copy-start.1 = (bf16[2,384,512]{2,1,0:T(8,128)(2,1)S(1)}, bf16[2,384,512]{2,1,0:T(8,128)(2,1)}, u32[]{:S(2)}) copy-start(bf16[2,384,512]{2,1,0:T(8,128)(2,1)} %constant.8.clone.back_tab) | copy-start | bytes 2359300
  3.0 1.1 %copy-start.2 = (bf16[2,512,384]{2,1,0:T(8,128)(2,1)S(1)}, bf16[2,512,384]{2,1,0:T(8,128)(2,1)}, u32[]{:S(2)}) copy-start(bf16[2,512,384]{2,1,0:T(8,128)(2,1)} %constant.7.clone.fwd_tab) | copy-start | bytes 2359300
  4.2 1.0 %copy-start.3 = (bf16[4,256,256]{2,1,0:T(8,128)(2,1)S(1)}, bf16[4,256,256]{2,1,0:T(8,128)(2,1)}, u32[]{:S(2)}) copy-start(bf16[4,256,256]{2,1,0:T(8,128)(2,1)} %constant.6.clone.plane_tab) | copy-start | bytes 1572868
  5.2 0.9 copy-start.4
  6.1 0.9 copy-start.5
  7.0 0.8 copy-start.6
  7.8 0.8 copy-start.7
  8.6 0.8 copy-start.8
  9.4 0.7 copy-start.9
where the time goes:
time: 91.5 us; the launch traced here: 90.9 us
  Pallas kernels  79.7 us (87%)
  local copies, waits for them, and re-layouts  10.6 us (12%)
    pallas_call x1, Pallas kernels, local(): pl.pallas_call(kernel, out_shape=(jax.ShapeDtypeStruct((2, 1, K, SL), F32...  79.7 us
    unnamed x22, local copies, waits for them, and re-layouts  10.6 us

commit v1 on v0

v1 whole, which is shorter than its diff:
```python
import functools
import math

import jax
import jax.numpy as jnp
import numpy as np
from jax import lax
from jax.experimental import pallas as pl
from jax.experimental.pallas import tpu as pltpu
from jax.sharding import PartitionSpec as P

MESH = pl.DeviceIdType.MESH
F32 = jnp.float32
BF16 = jnp.bfloat16
G = 192
GP = 256
L = 96
K = 96
SL = 128
NF = 32
NB = 16
PL = 6
CP = 12
CPP = 16
NC = 4
CS = 1024
CD = 8
A = 72
Q = 24


def halves(table):
    hi = table.astype(jnp.bfloat16)
    lo = (table - hi.astype(np.float64)).astype(jnp.bfloat16)
    return hi, lo


def three_beside(table):
    hi, lo = halves(table)
    return np.concatenate([hi, lo, hi], axis=1)


def three_below(table):
    hi, lo = halves(table)
    return np.concatenate([hi, hi, lo], axis=0)


def tables():
    f = np.arange(G)
    angle = 2.0 * math.pi * ((f[:, None] * f[None, :]) % G) / G
    cos, sin = np.cos(angle), np.sin(angle)
    plane_cos = np.zeros((GP, GP))
    plane_sin = np.zeros((GP, GP))
    plane_cos[:G, :G] = cos
    plane_sin[:G, :G] = sin
    forward = np.zeros((NF, CPP, 2, G))
    for part in range(2):
        rows = slice(part * PL, part * PL + PL)
        by_owner_cos = cos.reshape(NF, PL, G)
        by_owner_sin = sin.reshape(NF, PL, G)
        forward[:, rows, 0] = by_owner_sin if part else by_owner_cos
        forward[:, rows, 1] = by_owner_cos if part else -by_owner_sin
    forward = forward.reshape(NF * CPP, 2 * G)
    back = np.ascontiguousarray(forward.T)
    plane = three_below(np.concatenate([plane_cos, plane_sin], axis=1))
    order = np.concatenate([f[0::2], f[1::2]])
    lines = np.concatenate([plane_cos[order], plane_sin[order], plane_cos[order]], axis=0)
    return plane, np.stack(halves(lines)), three_beside(forward), three_beside(back)


def split(value):
    hi = value.astype(BF16)
    lo = (value - hi.astype(F32)).astype(BF16)
    return hi, lo


def dot(a, b):
    return jnp.dot(a, b, preferred_element_type=F32)


def dot_nt(a, b):
    return lax.dot_general(a, b, (((1,), (1,)), ((), ())), preferred_element_type=F32)


def abreast(value):
    hi, lo = split(value)
    return jnp.concatenate([hi, lo, hi], axis=1)


def stacked(value):
    hi, lo = split(value)
    return jnp.concatenate([hi, hi, lo], axis=0)


def kernel(
    wave_in,
    corr_in,
    kinetic_in,
    zslots_in,
    sticks_in,
    xline_in,
    pot_in,
    plane_in,
    x_in,
    fwd_in,
    back_in,
    h_out,
    red_out,
    wave,
    kinetic,
    zslots,
    sticks,
    xline,
    pot,
    plane_tab,
    x_tab,
    fwd_tab,
    back_tab,
    in_sem,
    send1,
    recv1,
    send2,
    recv2,
    dense,
    corr_all,
    potr,
    qt,
    rows,
    lhs,
    acc,
    s1,
    xf,
    xb,
    s3,
    ob,
    o4,
    back,
    fsum,
    bsum,
    s1_send,
    s1_recv,
    s2_send,
    s2_recv,
    up_send,
    up_recv,
    dn_send,
    dn_recv,
    f_send,
    f_recv,
    b_send,
    b_recv,
):
    band = lax.axis_index("band")
    fft = lax.axis_index("fft")
    barrier = pltpu.get_barrier_semaphore()

    def to_fft(d):
        return {"fft": d}

    def to_band(d):
        return {"band": d}

    loads = [
        pltpu.make_async_copy(src, dst, in_sem.at[n])
        for n, (src, dst) in enumerate(
            (
                (zslots_in, zslots),
                (wave_in, wave),
                (fwd_in, fwd_tab),
                (corr_in.at[:, 0], corr_all.at[band]),
                (sticks_in, sticks),
                (pot_in, pot.at[pl.ds(0, PL)]),
                (xline_in, xline),
                (plane_in, plane_tab),
                (x_in, x_tab),
                (kinetic_in, kinetic),
                (back_in, back_tab),
            )
        )
    ]
    for load in loads:
        load.start()

    recv2[...] = jnp.zeros(recv2.shape, F32)

    def greet_fft(t, carry):
        d = lax.rem(fft + t, NF)
        pl.semaphore_signal(barrier, inc=1, device_id=to_fft(d), device_id_type=MESH)
        return carry

    def greet_band(t, carry):
        d = lax.rem(band + t, NB)
        pl.semaphore_signal(barrier, inc=1, device_id=to_band(d), device_id_type=MESH)
        return carry

    lax.fori_loop(1, NF, greet_fft, 0)
    lax.fori_loop(1, NB, greet_band, 0)

    loads[0].wait()
    loads[1].wait()

    def z_half(start):
        iota = lax.broadcasted_iota(jnp.int32, (G // 2, SL), 0) + start

        def step(k, carry):
            re, im = carry
            row = zslots[pl.ds(k, 1), :]
            hit = iota == row
            re = jnp.where(hit, wave[0, 0, pl.ds(k, 1), :], re)
            im = jnp.where(hit, wave[1, 0, pl.ds(k, 1), :], im)
            return re, im

        zero = jnp.zeros((G // 2, SL), F32)
        re, im = lax.fori_loop(0, K, step, (zero, zero), unroll=4)
        dense[pl.ds(start, G // 2), :] = re
        dense[pl.ds(G + start, G // 2), :] = im

    z_half(0)
    z_half(G // 2)
    loads[2].wait()
    send1[...] = dot(fwd_tab[...], stacked(dense[...])).reshape(NF, CPP, SL)

    pl.semaphore_wait(barrier, NF - 1 + NB - 1)

    def copy1(dst, src):
        return pltpu.make_async_remote_copy(
            src_ref=send1.at[dst, pl.ds(0, CP)],
            dst_ref=recv1.at[src, pl.ds(0, CP)],
            send_sem=s1_send.at[dst],
            recv_sem=s1_recv.at[src],
            device_id=to_fft(dst),
            device_id_type=MESH,
        )

    def copy2(dst, src):
        return pltpu.make_async_remote_copy(
            src_ref=send2.at[dst, pl.ds(0, CP)],
            dst_ref=recv2.at[src, pl.ds(0, CP)],
            send_sem=s2_send.at[dst],
            recv_sem=s2_recv.at[src],
            device_id=to_fft(dst),
            device_id_type=MESH,
        )

    def send_one(t, carry):
        copy1(lax.rem(fft + t, NF), fft).start()
        return carry

    lax.fori_loop(1, NF, send_one, 0)
    recv1[fft] = send1[fft]

    above = lax.rem(band + 1, NB)
    below = lax.rem(band + NB - 1, NB)

    def ring_copy(up, t, part):
        slot = lax.rem(band + NB + 1 - t, NB) if up else lax.rem(band + t - 1, NB)
        return pltpu.make_async_remote_copy(
            src_ref=corr_all.at[slot, part],
            dst_ref=corr_all.at[slot, part],
            send_sem=(up_send if up else dn_send).at[t - 1, part],
            recv_sem=(up_recv if up else dn_recv).at[t - 1, part],
            device_id=to_band(above if up else below),
            device_id_type=MESH,
        )

    def ring(t, part):
        for up in (True, False):
            last = 8 if up == (part == 0) else 7
            if isinstance(t, int):
                if 1 < t <= last + 1:
                    ring_copy(up, t - 1, part).wait_recv()
                if t <= last:
                    ring_copy(up, t, part).start()
            else:
                ring_copy(up, t - 1, part).wait_recv()
                ring_copy(up, t, part).start()

    loads[3].wait()
    ring(1, 0)
    ring(1, 1)
    for load in loads[4:]:
        load.wait()

    def hot(condition):
        return jnp.where(condition, 1.0, 0.0).astype(BF16)

    cell_iota = lax.broadcasted_iota(jnp.int32, (GP, CS), 0)
    for n in range(NC):
        span = slice(n * CS, n * CS + CS)
        line = sticks[0:1, span]
        y = sticks[1:2, span]
        top = y < SL
        rows[n] = jnp.where(top, line >> 1, 2 * Q + (line >> 2))
        lane = jnp.where(top, (line & 1) * SL + y, (line & 3) * (SL // 2) + y - SL)
        qt[n] = hot(cell_iota == lane)

    def relay(q, carry):
        for j in range(3):
            potr[j, pl.ds(pl.multiple_of(q * 8, 8), 8), :] = pot[
                :, pl.ds(pl.multiple_of((q * 3 + j) * SL, SL), SL)
            ]
        return carry

    lax.fori_loop(0, G // 2, relay, 0, unroll=4)

    spot = lax.broadcasted_iota(jnp.int32, (L, GP), 1)
    kind = jnp.where(spot >= Q, 1, 0) + jnp.where(spot >= 2 * Q, 1, 0) + jnp.where(spot >= 3 * Q, 1, 0)
    order = hot(lax.broadcasted_iota(jnp.int32, (L, GP), 0) == 4 * (spot - Q * kind) + kind)
    pick = dot(hot(lax.broadcasted_iota(jnp.int32, (GP, L), 0) == xline[...]), order)
    pick_a = pick[:, :SL].astype(BF16)
    pick_t = jnp.transpose(pick[:, :SL])[:L].astype(BF16)
    first = lax.broadcasted_iota(jnp.int32, (L, 2 * G), 1) < G
    for n in range(2):
        xc = dot(x_tab[n, 0:G], pick_a).astype(BF16)
        xs = dot(x_tab[n, G : 2 * G], pick_a).astype(BF16)
        re = jnp.concatenate([xc, -xs], axis=1)
        im = jnp.concatenate([xs, xc], axis=1)
        yr = dot_nt(pick_t, x_tab[n, 0 : 2 * G]).astype(BF16)
        yi = dot_nt(pick_t, x_tab[n, G : 3 * G])
        yi = jnp.where(first, -yi, yi).astype(BF16)
        for k in (0, 2) if n == 0 else (1,):
            xf[0:G, k * GP : k * GP + GP] = re
            xf[G:, k * GP : k * GP + GP] = im
            xb[0:L, k * 2 * G : (k + 1) * 2 * G] = yr
            xb[L:, k * 2 * G : (k + 1) * 2 * G] = yi

    my_chunk = fft // CD
    a_iota = lax.broadcasted_iota(jnp.int32, (A, GP), 0)
    for n in range(NC):
        chunk = lax.rem(my_chunk + n, NC)

        def arrive(t, carry):
            src = chunk * CD + t

            @pl.when(src != fft)
            def _():
                copy1(src, src).wait_recv()

            return carry

        lax.fori_loop(0, CD, arrive, 0)
        for i in range(CD // 2):
            src = chunk * CD + 2 * i
            x = jnp.concatenate([recv1[src], recv1[src + 1]], axis=1)
            hi, lo = split(x)
            hi = hi.astype(F32)
            lo = lo.astype(F32)
            here = a_iota == rows[chunk][:, i * GP : i * GP + GP]
            for cp in range(0, CP, 2):
                at = slice(cp * A, cp * A + 2 * A)
                for j, v in enumerate((hi, lo)):
                    two = [jnp.where(here, v[cp + k : cp + k + 1], 0.0) for k in range(2)]
                    k = (j * CD // 2 + i) * GP
                    lhs[n % 2, at, k : k + GP] = jnp.concatenate(two, axis=0).astype(BF16)
        q = qt[chunk]
        cells = dot_nt(lhs[n % 2], jnp.concatenate([q, q], axis=1))
        for h in range(2):
            half = cells[:, h * SL : h * SL + SL]
            if n == 0:
                acc[h] = half
            else:
                acc[h] += half
        ring(2 + n // 2, n % 2)

    def line_block(cp):
        blocks = []
        for m in range(4):
            top = acc[m % 2, pl.ds(cp * A + m // 2, Q, stride=2), :]
            low = acc[m // 2, cp * A + 2 * Q : cp * A + A, :]
            if m % 2:
                low = pltpu.roll(low, SL // 2, 1)
            blocks.append(jnp.concatenate([top, low], axis=1))
        return jnp.concatenate(blocks, axis=0)

    third = 3 * L
    for k in range(6):
        s1[:, k * SL + L : k * SL + SL] = jnp.zeros((2, SL - L, 3 * GP), BF16)
    for n in range(2):
        planes = range(3 * n, 3 * n + 3)
        a = jnp.concatenate([line_block(c * PL + p) for c in range(2) for p in planes], axis=0)
        uv = dot(abreast(a), plane_tab[...])
        u, v = uv[:, :GP], uv[:, GP:]
        re = split(u[:third] - v[third:])
        im = split(v[:third] + u[third:])
        for i in range(3):
            at = slice(i * L, i * L + L)
            for k in range(3):
                s1[n, k * GP : k * GP + L, i * GP : i * GP + GP] = re[k // 2][at]
                s1[n, k * GP + SL : k * GP + SL + L, i * GP : i * GP + GP] = im[k // 2][at]
        ring(4, n)

    for n in range(2):
        r = dot(xf[...], s1[n])
        parts = []
        for i in range(3):
            v = [potr[j, pl.ds(3 * n + i, G // 2, stride=8), :] for j in range(3)]
            w = pltpu.roll(jnp.concatenate(v, axis=1), G, 1)
            v = jnp.concatenate([jnp.concatenate(v[:2], axis=1), w[:, :GP]], axis=0)
            parts.append(r[:, i * GP : i * GP + GP] * jnp.concatenate([v, v], axis=0))
        s3[n] = dot(xb[...], stacked(jnp.concatenate(parts, axis=1)))
        ring(5 + n, 0)
        ring(5 + n, 1)

    low_lane = lax.broadcasted_iota(jnp.int32, (Q, SL), 1) < SL // 2
    for n in range(2):
        a = jnp.concatenate([s3[n, :, i * GP : i * GP + GP] for i in range(3)], axis=0)
        uv = dot(abreast(a), plane_tab[...])
        u, v = uv[:, :GP], uv[:, GP:]
        for i in range(3):
            top = slice(2 * i * L, 2 * i * L + L)
            low = slice(2 * i * L + L, 2 * i * L + 2 * L)
            for c, lines in enumerate((u[top] + v[low], u[low] - v[top])):
                cp = c * PL + 3 * n + i
                block = [lines[m * Q : m * Q + Q] for m in range(4)]
                for m in range(4):
                    ob[m % 2, pl.ds(cp * A + m // 2, Q, stride=2), :] = block[m][:, :SL]
                for h in range(2):
                    ob[h, cp * A + 2 * Q : cp * A + A, :] = jnp.where(
                        low_lane,
                        block[2 * h][:, SL:],
                        pltpu.roll(block[2 * h + 1][:, SL:], SL // 2, 1),
                    )
        ring(7, n)
    hi, lo = split(jnp.concatenate([ob[0], ob[1]], axis=1))
    o4[:, :GP] = hi
    o4[:, GP:] = lo

    def gather_step(n, carry):
        chunk = lax.rem(my_chunk + n, NC)
        for i in range(CD // 2):
            span = slice(i * GP, i * GP + GP)
            q = qt[chunk, :, span]
            here = a_iota == rows[chunk][:, span]
            full = dot(o4[...], jnp.concatenate([q, q], axis=0))
            for cp in range(CP):
                v = jnp.where(here, full[cp * A : cp * A + A], 0.0)
                v = jnp.sum(v, axis=0, keepdims=True)
                send2[chunk * CD + 2 * i, cp : cp + 1, :] = v[:, :SL]
                send2[chunk * CD + 2 * i + 1, cp : cp + 1, :] = v[:, SL:]

        def leave(t, inner):
            dst = chunk * CD + t

            @pl.when(dst != fft)
            def _():
                copy2(dst, fft).start()

            return inner

        return lax.fori_loop(0, CD, leave, carry)

    lax.fori_loop(1, 3, gather_step, 0)
    ring(8, 0)
    lax.fori_loop(3, NC + 1, gather_step, 0)
    ring(8, 1)
    recv2[fft, 0:CP] = send2[fft, 0:CP]

    def wait_two(t, carry):
        src = lax.rem(fft + t, NF)
        copy2(src, src).wait_recv()
        return carry

    lax.fori_loop(1, NF, wait_two, 0)

    back[...] = dot(back_tab[...], stacked(recv2[...].reshape(NF * CPP, SL)))
    zs = zslots[...]

    def pick_step(z, carry):
        re, im = carry
        hit = zs == z
        re = jnp.where(hit, back[pl.ds(z, 1), :], re)
        im = jnp.where(hit, back[pl.ds(G + z, 1), :], im)
        return re, im

    zero = jnp.zeros((K, SL), F32)
    v_re, v_im = lax.fori_loop(0, G, pick_step, (zero, zero), unroll=4)
    scale = 1.0 / float(G) ** 3
    kin = kinetic[...]
    h_re = kin * wave[0, 0] + v_re * scale
    h_im = kin * wave[1, 0] + v_im * scale
    h_out[0, 0] = h_re
    h_out[1, 0] = h_im

    ring(9, 0)
    ring(9, 1)
    row_iota = lax.broadcasted_iota(jnp.int32, (2 * NB, SL), 0)

    def contract(i, total):
        c_re = corr_all[i, 0]
        c_im = corr_all[i, 1]
        re = jnp.sum(c_re * h_re + c_im * h_im, axis=0, keepdims=True)
        im = jnp.sum(c_re * h_im - c_im * h_re, axis=0, keepdims=True)
        total = jnp.where(row_iota == i, re, total)
        return jnp.where(row_iota == NB + i, im, total)

    total = lax.fori_loop(0, NB, contract, jnp.zeros((2 * NB, SL), F32))
    column = jnp.sum(total, axis=1, keepdims=True)
    lane_iota = lax.broadcasted_iota(jnp.int32, (2 * NB, SL), 1)
    mine = jnp.sum(jnp.where(row_iota == lane_iota, column, 0.0), axis=0, keepdims=True)
    fsum[fft] = mine

    def f_copy(dst, src):
        return pltpu.make_async_remote_copy(
            src_ref=fsum.at[src],
            dst_ref=fsum.at[src],
            send_sem=f_send.at[dst],
            recv_sem=f_recv.at[src],
            device_id=to_fft(dst),
            device_id_type=MESH,
        )

    def b_copy(dst, src):
        return pltpu.make_async_remote_copy(
            src_ref=bsum.at[src],
            dst_ref=bsum.at[src],
            send_sem=b_send.at[dst],
            recv_sem=b_recv.at[src],
            device_id=to_band(dst),
            device_id_type=MESH,
        )

    def f_start(t, carry):
        f_copy(lax.rem(fft + t, NF), fft).start()
        return carry

    def f_wait(t, carry):
        src = lax.rem(fft + t, NF)
        f_copy(src, src).wait_recv()
        return carry

    lax.fori_loop(1, NF, f_start, 0)
    lax.fori_loop(1, NF, f_wait, 0)
    bsum[band] = jnp.sum(fsum[...], axis=0)

    def b_start(t, carry):
        b_copy(lax.rem(band + t, NB), band).start()
        return carry

    def b_wait(t, carry):
        src = lax.rem(band + t, NB)
        b_copy(src, src).wait_recv()
        return carry

    lax.fori_loop(1, NB, b_start, 0)
    lax.fori_loop(1, NB, b_wait, 0)

    block = bsum[...].reshape(NB, SL)
    root = 1.0 / math.sqrt(NF * SL * K)
    b_row = lax.broadcasted_iota(jnp.int32, (NB, SL), 0)
    b_lane = lax.broadcasted_iota(jnp.int32, (NB, SL), 1)
    for part in range(2):
        column = jnp.sum(
            jnp.where(b_lane == part * NB + band, block, 0.0), axis=1, keepdims=True
        )
        line = jnp.sum(jnp.where(b_row == b_lane, column, 0.0), axis=0, keepdims=True)
        red_out[part] = line[:, :NB] * root

    def drain(t, carry):
        d = lax.rem(fft + t, NF)
        copy1(d, fft).wait_send()
        copy2(d, fft).wait_send()
        f_copy(d, fft).wait_send()
        return carry

    lax.fori_loop(1, NF, drain, 0)

    def drain_band(t, carry):
        b_copy(lax.rem(band + t, NB), band).wait_send()
        return carry

    lax.fori_loop(1, NB, drain_band, 0)
    for part in range(2):
        for up in (True, False):
            for t in range(1, 9 if up == (part == 0) else 8):
                ring_copy(up, t, part).wait_send()


def local(wave, corr, kinetic, zslots, sticks, xlines, pot):
    plane, lines, forward, back = tables()
    dma = pltpu.SemaphoreType.DMA
    vmem = pltpu.VMEM
    return pl.pallas_call(
        kernel,
        out_shape=(
            jax.ShapeDtypeStruct((2, 1, K, SL), F32),
            jax.ShapeDtypeStruct((2, 1, NB), F32),
        ),
        in_specs=[pl.BlockSpec(memory_space=pltpu.HBM)] * 11,
        out_specs=(pl.BlockSpec(memory_space=vmem),) * 2,
        scratch_shapes=[
            vmem((2, 1, K, SL), F32),
            vmem((K, SL), F32),
            vmem((K, SL), jnp.int32),
            vmem((2, NF * SL), jnp.int32),
            vmem((1, L), jnp.int32),
            vmem((8, G * G), F32),
            vmem(plane.shape, BF16),
            vmem(lines.shape, BF16),
            vmem(forward.shape, BF16),
            vmem(back.shape, BF16),
            dma((11,)),
            vmem((NF, CPP, SL), F32),
            vmem((NF, CPP, SL), F32),
            vmem((NF, CPP, SL), F32),
            vmem((NF, CPP, SL), F32),
            vmem((2 * G, SL), F32),
            vmem((NB, 2, K, SL), F32),
            vmem((3, 4 * G, SL), F32),
            vmem((NC, GP, CS), BF16),
            vmem((NC, 1, CS), jnp.int32),
            vmem((2, CP * A, 2 * CS), BF16),
            vmem((2, CP * A, SL), F32),
            vmem((2, 3 * GP, 3 * GP), BF16),
            vmem((2 * G, 3 * GP), BF16),
            vmem((2 * L, 6 * G), BF16),
            vmem((2, 2 * L, 3 * GP), F32),
            vmem((2, CP * A, SL), F32),
            vmem((CP * A, 2 * GP), BF16),
            vmem((2 * G, SL), F32),
            vmem((NF, 1, SL), F32),
            vmem((NB, 1, SL), F32),
            dma((NF,)),
            dma((NF,)),
            dma((NF,)),
            dma((NF,)),
            dma((8, 2)),
            dma((8, 2)),
            dma((8, 2)),
            dma((8, 2)),
            dma((NF,)),
            dma((NF,)),
            dma((NB,)),
            dma((NB,)),
        ],
        compiler_params=pltpu.CompilerParams(
            collective_id=0,
            has_side_effects=True,
            vmem_limit_bytes=48 * 1024 * 1024,
        ),
    )(
        wave,
        corr,
        kinetic,
        zslots,
        sticks,
        xlines.reshape(1, L),
        pot,
        jnp.asarray(plane),
        jnp.asarray(lines),
        jnp.asarray(forward),
        jnp.asarray(back),
    )


def solution(mesh):
    return jax.shard_map(
        local,
        mesh=mesh,
        in_specs=(
            P(None, "band", None, "fft"),
            P(None, "band", None, "fft"),
            P(None, "fft"),
            P(None, "fft"),
            P(),
            P(),
            P("fft", None),
        ),
        out_specs=(P(None, "band", None, "fft"), P(None, "band", None)),
        check_vma=False,
    )
```

time: 91.5 us -> 83.5 us (0.913)
  Pallas kernels: 79.7 us -> 70.3 us
  local copies, waits for them, and re-layouts: 10.6 us -> 12 us
    pallas_call x1, Pallas kernels: 79.7 us -> 70.3 us  [local(): pl.pallas_call(kernel, out_shape=(jax.ShapeDtypeStruct((2, 1, K, SL), F32...]
    unnamed x22 -> x24, local copies, waits for them, and re-layouts: 10.6 us -> 12 us
where the time goes in v1:
time: 83.5 us; the launch traced here: 82.9 us
  Pallas kernels  70.3 us (84%)
  local copies, waits for them, and re-layouts  12 us (14%)
    pallas_call x1, Pallas kernels, local(): pl.pallas_call(kernel, out_shape=(jax.ShapeDtypeStruct((2, 1, K, SL), F32...  70.3 us
    unnamed x24, local copies, waits for them, and re-layouts  12 us

profile of v1, /device:TPU:1, one launch (start us, length us, event | category | flops | bytes accessed | tf_op | source)
XLA Modules:
  0.0 82.9 jit_solution(6080404367773099235)
XLA Ops:
  0.6 0.0 copy-start
  0.6 1.3 %copy-done = f32[6,36864]{1,0:T(8,128)S(1)} copy-done((f32[6,36864]{1,0:T(8,128)S(1)}, f32[6,36864]{1,0:T(8,128)}, u32[]{:S(2)}) %copy-start) | copy-done | bytes 884760
  1.9 0.0 copy-start.1
  1.9 1.3 %copy-done.1 = bf16[384,1536]{1,0:T(8,128)(2,1)S(1)} copy-done((bf16[384,1536]{1,0:T(8,128)(2,1)S(1)}, bf16[384,1536]{1,0:T(8,128)(2,1)}, u32[]{:S(2)}) %copy-start.1) | copy-done | bytes 1179672
  3.2 0.0 copy-start.2
  3.2 1.3 %copy-done.2 = bf16[512,1152]{1,0:T(8,128)(2,1)S(1)} copy-done((bf16[512,1152]{1,0:T(8,128)(2,1)S(1)}, bf16[512,1152]{1,0:T(8,128)(2,1)}, u32[]{:S(2)}) %copy-start.2) | copy-done | bytes 1179672
  4.4 0.0 copy-start.3
  4.4 1.1 %copy-done.3 = bf16[768,512]{1,0:T(8,128)(2,1)S(1)} copy-done((bf16[768,512]{1,0:T(8,128)(2,1)S(1)}, bf16[768,512]{1,0:T(8,128)(2,1)}, u32[]{:S(2)}) %copy-start.3) | copy-done | bytes 786456
  5.6 0.0 copy-start.4
  5.6 1.1 %copy-done.4 = bf16[2,576,256]{2,1,0:T(8,128)(2,1)S(1)} copy-done((bf16[2,576,256]{2,1,0:T(8,128)(2,1)S(1)}, bf16[2,576,256]{2,1,0:T(8,128)(2,1)}, u32[]{:S(2)}) %copy-start.4) | copy-done | bytes 589848
  6.6 0.0 copy-start.5
  6.6 0.9 %copy-done.5 = f32[2,1,96,128]{3,2,1,0:T(8,128)S(1)} copy-done((f32[2,1,96,128]{3,2,1,0:T(8,128)S(1)}, f32[2,1,96,128]{3,2,1,0:T(8,128)}, u32[]{:S(2)}) %copy-start.5) | copy-done | bytes 98328
  7.5 0.0 copy-start.6
  7.5 0.9 %copy-done.6 = f32[2,1,96,128]{3,2,1,0:T(8,128)S(1)} copy-done((f32[2,1,96,128]{3,2,1,0:T(8,128)S(1)}, f32[2,1,96,128]{3,2,1,0:T(8,128)}, u32[]{:S(2)}) %copy-start.6) | copy-done | bytes 98328
  8.4 0.0 copy-start.7
  8.4 0.8 copy-done.7
  9.2 0.0 copy-start.8
  9.2 0.8 copy-done.8
  10.0 0.0 copy-start.9
  10.0 0.8 copy-done.9
  10.8 0.0 copy-start.10
  10.8 0.7 copy-done.10
  11.4 70.3 %shard_map.122 = (f32[2,1,96,128]{3,2,1,0:T(8,128)S(1)}, f32[2,1,16]{2,1,0:T(1,128)S(1)}) custom-call(f32[2,1,96,128]{3,2,1,0:T(8,128)S(1)} %copy-done.5, f32[2,1,96,128]{3,2,1,0:T(8,128)S(1)} %copy-done.6, f32[96,128]{1,0:T(8,128)S(1)} %copy-done.7, s32[96,128]{1,0:T(8,128)S(1)} %copy-done.8, s32[2,4096]{1,0:T(2,128)S(1)} %copy-done.9, ...), custom_call_target="tpu_custom_call" | custom-call | tf_op jit(solution)/shard_map/pallas_call | solution.py:582
  81.7 0.6 copy.15
  82.4 0.6 copy.16
Async XLA Ops:
  0.6 1.3 %copy-start = (f32[6,36864]{1,0:T(8,128)S(1)}, f32[6,36864]{1,0:T(8,128)}, u32[]{:S(2)}) copy-start(f32[6,36864]{1,0:T(8,128)} %pot_in.1) | copy-start | bytes 2654212
  1.9 1.3 %copy-start.1 = (bf16[384,1536]{1,0:T(8,128)(2,1)S(1)}, bf16[384,1536]{1,0:T(8,128)(2,1)}, u32[]{:S(2)}) copy-start(bf16[384,1536]{1,0:T(8,128)(2,1)} %constant.11.clone.back_in) | copy-start | bytes 3538948
  3.2 1.3 %copy-start.2 = (bf16[512,1152]{1,0:T(8,128)(2,1)S(1)}, bf16[512,1152]{1,0:T(8,128)(2,1)}, u32[]{:S(2)}) copy-start(bf16[512,1152]{1,0:T(8,128)(2,1)} %constant.10.clone.fwd_in) | copy-start | bytes 3538948
  4.4 1.1 %copy-start.3 = (bf16[768,512]{1,0:T(8,128)(2,1)S(1)}, bf16[768,512]{1,0:T(8,128)(2,1)}, u32[]{:S(2)}) copy-start(bf16[768,512]{1,0:T(8,128)(2,1)} %constant.8.clone.plane_in) | copy-start | bytes 2359300
  5.6 1.1 %copy-start.4 = (bf16[2,576,256]{2,1,0:T(8,128)(2,1)S(1)}, bf16[2,576,256]{2,1,0:T(8,128)(2,1)}, u32[]{:S(2)}) copy-start(bf16[2,576,256]{2,1,0:T(8,128)(2,1)} %constant.9.clone.x_in) | copy-start | bytes 1769476
  6.6 0.9 %copy-start.5 = (f32[2,1,96,128]{3,2,1,0:T(8,128)S(1)}, f32[2,1,96,128]{3,2,1,0:T(8,128)}, u32[]{:S(2)}) copy-start(f32[2,1,96,128]{3,2,1,0:T(8,128)} %wave_in.1) | copy-start | bytes 294916
  7.5 0.9 %copy-start.6 = (f32[2,1,96,128]{3,2,1,0:T(8,128)S(1)}, f32[2,1,96,128]{3,2,1,0:T(8,128)}, u32[]{:S(2)}) copy-start(f32[2,1,96,128]{3,2,1,0:T(8,128)} %corr_in.1) | copy-start | bytes 294916
  8.4 0.8 copy-start.7
  9.2 0.8 copy-start.8
  10.0 0.8 copy-start.9
  10.8 0.7 copy-start.10
